TPU v7x, 32 devices: a whole 2x2x4 slice. The times are simulated.
32 devices in a mesh: energy: 8 (over y, x, core), space: 4 (over z).
Axes of the slice: x: 2, y: 2, z: 4, core: 2. Of those that a mesh axis runs over, the one named last changes fastest.
Arguments:
- chain_map: float32 [2, 1536, 384], P(None, 'space'), may hold values from -0.21875 to 0.21875
- chain_source: float32 [2, 256, 1536], P(None, 'energy', 'space'), may hold values from -4 to 4
- local_map: float32 [2, 1536, 768], P(None, 'space'), may hold values from -0.21875 to 0.21875
- local_source: float32 [2, 3072, 256], P(None, 'space', 'energy'), may hold values from -6 to 6
- interaction: float32 [2, 4096, 256], P(None, 'space', 'energy'), may hold values from -6 to 6
- element_pairs: int32 [2, 4096], P(None, 'space'), may hold values from 0 to 767, as said below
Outputs:
- self_energy: float32 [2, 4096, 256], P(None, 'space', 'energy')
Inputs may be any that keep to these rules, and one draw needn't show every extreme that they name: `element_pairs`: both orbitals of a selected element lie in the same block of 384 orbitals or in neighbouring blocks of its partition.
All inputs are finite; a program needn't handle non-finite values.
Results may differ from a plain program's by a relative error of at most 0.00011.
Values sent between devices are 32-bit elements; how exact they have to be, the bound alone decides.
A program may use at most 64 MiB of HBM per device.

v0:
```python
import math

import jax
import jax.numpy as jnp
from jax import lax
from jax.sharding import PartitionSpec as P

highest = lax.Precision.HIGHEST


def shifted_2(x, axis, by):
    length = lax.axis_size(axis)
    pairs = [(i, i + by) for i in range(length) if 0 <= i + by < length]
    return lax.ppermute(x, axis, pairs)


def stacked_coupling(coupling):
    upper = jnp.concatenate([coupling[0], coupling[1]], axis=1)
    lower = jnp.concatenate([-coupling[1], coupling[0]], axis=1)
    return jnp.concatenate([upper, lower], axis=0)


def stacked_step(states, coupled, sources):
    width = states.shape[2]
    joined = jnp.concatenate([states[0], states[1]], axis=1)
    product = jnp.dot(joined, coupled, precision=highest, preferred_element_type=jnp.float32)
    return jnp.stack([product[:, :width], product[:, width:]]) + sources


def spread_dot(weights, states):
    count = states.shape[1]
    width = weights.shape[1]
    stacked_weights = weights.reshape(2 * width, weights.shape[2])
    upper = jnp.concatenate([states[0].T, states[1].T], axis=1)
    lower = jnp.concatenate([-states[1].T, states[0].T], axis=1)
    stacked_states = jnp.concatenate([upper, lower], axis=0)
    product = lax.dot_general(
        stacked_weights,
        stacked_states,
        (((0,), (0,)), ((), ())),
        precision=highest,
        preferred_element_type=jnp.float32,
    )
    return jnp.stack([product[:, :count], product[:, count:]])


def phase_table(row_count, col_count, period, direction):
    product = (
        lax.broadcasted_iota(jnp.int32, (row_count, col_count), 0)
        * lax.broadcasted_iota(jnp.int32, (row_count, col_count), 1)
        % period
    )
    angles = direction * 2.0 * math.pi / period * product.astype(jnp.float32)
    return (jnp.cos(angles), jnp.sin(angles))


def complex_einsum(pattern, left_pair, right_pair):

    def single(first_part, second_part):
        return jnp.einsum(
            pattern, first_part, second_part, precision=highest, preferred_element_type=jnp.float32
        )

    real_part = single(left_pair[0], right_pair[0]) - single(left_pair[1], right_pair[1])
    imag_part = single(left_pair[0], right_pair[1]) + single(left_pair[1], right_pair[0])
    return (real_part, imag_part)


def complex_times(left_pair, right_pair):
    real_part = left_pair[0] * right_pair[0] - left_pair[1] * right_pair[1]
    imag_part = left_pair[0] * right_pair[1] + left_pair[1] * right_pair[0]
    return (real_part, imag_part)


def split_sizes(length):
    inner_size = 128
    return (length // inner_size, inner_size)


def forward_transform(real_part, imag_part):
    length = real_part.shape[-1]
    outer_size, inner_size = split_sizes(length)
    sectioned = (
        real_part.reshape(-1, outer_size, inner_size),
        imag_part.reshape(-1, outer_size, inner_size),
    )
    sectioned = complex_einsum(
        "mab,ak->mkb", sectioned, phase_table(outer_size, outer_size, outer_size, -1.0)
    )
    sectioned = complex_times(sectioned, phase_table(outer_size, inner_size, length, -1.0))
    return complex_einsum(
        "mkb,bq->mkq", sectioned, phase_table(inner_size, inner_size, inner_size, -1.0)
    )


def inverse_transform(spectrum, length):
    outer_size, inner_size = split_sizes(length)
    sectioned = complex_einsum(
        "mkq,qb->mkb", spectrum, phase_table(inner_size, inner_size, inner_size, 1.0)
    )
    sectioned = complex_times(sectioned, phase_table(outer_size, inner_size, length, 1.0))
    sectioned = complex_einsum(
        "mkb,ka->mab", sectioned, phase_table(outer_size, outer_size, outer_size, 1.0)
    )
    return (sectioned[0].reshape(-1, length) / length, sectioned[1].reshape(-1, length) / length)


def correlate(pieces):
    lesser, screened = pieces
    layout = lesser.shape
    length = layout[-1]
    lesser_spec = forward_transform(lesser[0].reshape(-1, length), lesser[1].reshape(-1, length))
    screened_spec = forward_transform(
        screened[0].reshape(-1, length), screened[1].reshape(-1, length)
    )
    response_re, response_im = inverse_transform(complex_times(lesser_spec, screened_spec), length)
    factor = length ** (-0.5)
    response = jnp.stack([response_re * factor, response_im * factor]).reshape(layout)
    return lax.all_to_all(response, "energy", split_axis=3, concat_axis=1, tiled=True)


def body(chain_map, chain_source, local_map, local_source, interaction, element_pairs):
    coupled = stacked_coupling(chain_map)

    def advance(turn_index, carried):
        shifted = stacked_step(carried, coupled, chain_source)
        return shifted_2(shifted, "space", 1)

    incoming = lax.fori_loop(0, lax.axis_size("space") - 1, advance, jnp.zeros_like(chain_source))
    wavefunction = spread_dot(local_map, incoming) + local_source
    left_rows = jnp.take(wavefunction, element_pairs[0], axis=1)
    right_rows = jnp.take(wavefunction, element_pairs[1], axis=1)
    lesser_re = left_rows[0] * right_rows[0] + left_rows[1] * right_rows[1]
    lesser_im = left_rows[1] * right_rows[0] - left_rows[0] * right_rows[1]
    groups = lax.axis_size("energy")
    selected, energies = lesser_re.shape
    lesser = jnp.stack([lesser_re, lesser_im]).reshape(2, groups, selected // groups, energies)
    screened = interaction.reshape(2, groups, selected // groups, energies)
    self_energy = correlate(
        (
            lax.all_to_all(lesser, "energy", split_axis=1, concat_axis=3, tiled=True),
            lax.all_to_all(screened, "energy", split_axis=1, concat_axis=3, tiled=True),
        )
    )
    return self_energy.reshape(2, selected, energies)


def solution(mesh):
    in_specs = (
        P(None, "space", None),
        P(None, "energy", "space"),
        P(None, "space", None),
        P(None, "space", "energy"),
        P(None, "space", "energy"),
        P(None, "space"),
    )
    out_specs = P(None, "space", "energy")
    return jax.shard_map(body, mesh=mesh, in_specs=in_specs, out_specs=out_specs, check_vma=False)
```

profile of v0, /device:TPU:25, one launch (start us, length us, event | category | flops | bytes accessed | tf_op | source)
XLA Modules:
  0.0 104.6 jit_solution(1941587927598817450)
XLA Ops:
  0.0 2.5 %slice_bitcast_fusion.4 = (f32[384,384]{1,0:T(8,128)}, f32[384,384]{1,0:T(8,128)}) fusion(f32[2,384,384]{2,1,0:T(8,128)} %param.10), kind=kLoop, calls=%fused_computation.32 | loop fusion | bytes 2359296 | tf_op jit(solution)/shard_map/squeeze | solution.py:18
  2.6 0.0 copy-start.2
  2.6 3.1 %maximum_maximum_fusion = f32[768,768]{1,0:T(8,128)} fusion(f32[384,384]{1,0:T(8,128)} %get-tuple-element.44, f32[384,384]{1,0:T(8,128)S(1)} %fusion.205, f32[384,384]{1,0:T(8,128)} %get-tuple-element.43), kind=kLoop, calls=%fused_computation.12 | loop fusion | flops 1769472 | bytes 4128768 | tf_op jit(solution)/shard_map/concatenate | solution.py:20
  5.6 0.0 copy-start.4
  5.6 25.5 %while.10 = (s32[]{:T(128)}, f32[2,32,384]{2,1,0:T(8,128)S(1)}, f32[768,768]{1,0:T(8,128)}, f32[2,32,384]{2,1,0:T(8,128)S(1)}, s32[]{:T(128)}) while((s32[]{:T(128)}, f32[2,32,384]{2,1,0:T(8,128)S(1)}, f32[768,768]{1,0:T(8,128)}, f32[2,32,384]{2,1,0:T(8,128)S(1)}, s32[]{:T(128)}) %tuple.44), condition=%wide.region_1.0_spmd, body=%wide.region_0.0_spmd.sunk | while | flops 226566144 | bytes 3637349 | solution.py:129
  5.7 3.1 %fusion.231 = f32[32,768]{1,0:T(8,128)S(1)} fusion(f32[768,768]{1,0:T(8,128)} %get-tuple-element.116, f32[32,384]{1,0:T(8,128)S(1)} %get-tuple-element.100, f32[32,384]{1,0:T(8,128)S(1)} %get-tuple-element.101), kind=kOutput, calls=%fused_computation.2.clone.1 | convolution fusion | flops 226516992 | bytes 2555904 | tf_op jit(solution)/shard_map/while/body/eval_jaxpr/dot_general | solution.py:26
  8.8 1.3 %collective-permute-start = (f32[2,32,384]{2,1,0:T(8,128)S(1)}, f32[2,32,384]{2,1,0:T(8,128)S(1)}, u32[]{:S(2)}, u32[]{:S(2)}) collective-permute-start(f32[2,32,384]{2,1,0:T(8,128)S(1)} %maximum_add_fusion.3), channel_id=1, source_target_pairs={{0,1},{1,2},{2,3},{4,5},{5,6},{6,7},{8,9},{9,10},{10,11},{12,13},{... | collective-permute-start | bytes 294920 | tf_op jit(solution)/shard_map/while/body/eval_jaxpr/ppermute | solution.py:14
  10.1 4.1 %collective-permute-done = f32[2,32,384]{2,1,0:T(8,128)S(1)} collective-permute-done((f32[2,32,384]{2,1,0:T(8,128)S(1)}, f32[2,32,384]{2,1,0:T(8,128)S(1)}, u32[]{:S(2)}, u32[]{:S(2)}) %collective-permute-start) | collective-permute-done | bytes 98336 | tf_op jit(solution)/shard_map/while/body/eval_jaxpr/ppermute | solution.py:14
  14.2 3.1 %fusion.231 = f32[32,768]{1,0:T(8,128)S(1)} fusion(f32[768,768]{1,0:T(8,128)} %get-tuple-element.116, f32[32,384]{1,0:T(8,128)S(1)} %get-tuple-element.100, f32[32,384]{1,0:T(8,128)S(1)} %get-tuple-element.101), kind=kOutput, calls=%fused_computation.2.clone.1 | convolution fusion | flops 226516992 | bytes 2555904 | tf_op jit(solution)/shard_map/while/body/eval_jaxpr/dot_general | solution.py:26
  17.3 1.3 %collective-permute-start = (f32[2,32,384]{2,1,0:T(8,128)S(1)}, f32[2,32,384]{2,1,0:T(8,128)S(1)}, u32[]{:S(2)}, u32[]{:S(2)}) collective-permute-start(f32[2,32,384]{2,1,0:T(8,128)S(1)} %maximum_add_fusion.3), channel_id=1, source_target_pairs={{0,1},{1,2},{2,3},{4,5},{5,6},{6,7},{8,9},{9,10},{10,11},{12,13},{... | collective-permute-start | bytes 294920 | tf_op jit(solution)/shard_map/while/body/eval_jaxpr/ppermute | solution.py:14
  18.6 4.1 %collective-permute-done = f32[2,32,384]{2,1,0:T(8,128)S(1)} collective-permute-done((f32[2,32,384]{2,1,0:T(8,128)S(1)}, f32[2,32,384]{2,1,0:T(8,128)S(1)}, u32[]{:S(2)}, u32[]{:S(2)}) %collective-permute-start) | collective-permute-done | bytes 98336 | tf_op jit(solution)/shard_map/while/body/eval_jaxpr/ppermute | solution.py:14
  22.7 3.1 %fusion.231 = f32[32,768]{1,0:T(8,128)S(1)} fusion(f32[768,768]{1,0:T(8,128)} %get-tuple-element.116, f32[32,384]{1,0:T(8,128)S(1)} %get-tuple-element.100, f32[32,384]{1,0:T(8,128)S(1)} %get-tuple-element.101), kind=kOutput, calls=%fused_computation.2.clone.1 | convolution fusion | flops 226516992 | bytes 2555904 | tf_op jit(solution)/shard_map/while/body/eval_jaxpr/dot_general | solution.py:26
  25.8 1.3 %collective-permute-start = (f32[2,32,384]{2,1,0:T(8,128)S(1)}, f32[2,32,384]{2,1,0:T(8,128)S(1)}, u32[]{:S(2)}, u32[]{:S(2)}) collective-permute-start(f32[2,32,384]{2,1,0:T(8,128)S(1)} %maximum_add_fusion.3), channel_id=1, source_target_pairs={{0,1},{1,2},{2,3},{4,5},{5,6},{6,7},{8,9},{9,10},{10,11},{12,13},{... | collective-permute-start | bytes 294920 | tf_op jit(solution)/shard_map/while/body/eval_jaxpr/ppermute | solution.py:14
  27.1 4.1 %collective-permute-done = f32[2,32,384]{2,1,0:T(8,128)S(1)} collective-permute-done((f32[2,32,384]{2,1,0:T(8,128)S(1)}, f32[2,32,384]{2,1,0:T(8,128)S(1)}, u32[]{:S(2)}, u32[]{:S(2)}) %collective-permute-start) | collective-permute-done | bytes 98336 | tf_op jit(solution)/shard_map/while/body/eval_jaxpr/ppermute | solution.py:14
  31.3 1.5 %convolution_bitcast_fusion = f32[768,64]{0,1:T(8,128)S(1)} fusion(f32[768,768]{1,0:T(8,128)S(1)} %bitcast.163, f32[384,32]{0,1:T(8,128)S(1)} %get-tuple-element.60, f32[384,32]{0,1:T(8,128)S(1)} %fusion.204, f32[384,32]{0,1:T(8,128)S(1)} %get-tuple-element.59), kind=kOutput, calls=%fused_computation.13 | convolution fusion | flops 453132288 | bytes 2703360 | tf_op jit(solution)/shard_map/dot_general | solution.py:37
  32.9 0.5 copy.78
  33.4 7.5 %gather_fusion = f32[1024,2,32]{2,1,0:T(2,128)} fusion(f32[2,768,32]{2,0,1:T(2,128)S(1)} %copy.78, s32[1024]{0:T(1024)S(1)} %fusion.77), kind=kCustom, calls=%fused_computation.clone | custom fusion | bytes 528384 | tf_op jit(solution)/shard_map/jit(_take)/gather | solution.py:131
  40.9 7.5 %gather_fusion.1 = f32[1024,2,32]{2,1,0:T(2,128)} fusion(f32[2,768,32]{2,0,1:T(2,128)S(1)} %copy.78, s32[1024]{0:T(1024)S(1)} %fusion.78), kind=kCustom, calls=%fused_computation.1.clone | custom fusion | bytes 528384 | tf_op jit(solution)/shard_map/jit(_take)/gather | solution.py:132
  48.4 6.1 %select_bitcast_fusion = (f32[2,1024,32]{2,0,1:T(2,128)S(1)}, f32[2,1024,32]{2,0,1:T(2,128)S(1)}) fusion(f32[1024,2,32]{2,1,0:T(2,128)} %gather_fusion.1, pred[1024]{0:T(1024)(128)(4,1)S(1)} %compare_and_fusion, f32[1024,2,32]{2,1,0:T(2,128)} %gather_fusion, pred[1024]{0:T(1024)(128)(4,1)S(1)} %compare_and_fusion.1), kind=kLoop, calls=%fused_computation.30 | loop fusion | flops 131072 | bytes 1050624 | tf_op jit(solution)/shard_map/jit(_take)/select_n | solution.py:132
  54.5 1.4 %multiply_add_fusion = (f32[1,1024,32]{2,0,1:T(1,128)S(1)}, f32[1,1024,32]{2,0,1:T(1,128)S(1)}) fusion(f32[2,1024,32]{2,0,1:T(2,128)S(1)} %get-tuple-element.65, f32[2,1024,32]{2,0,1:T(2,128)S(1)} %get-tuple-element.66), kind=kLoop, calls=%fused_computation.35 | loop fusion | flops 196608 | bytes 786432 | tf_op jit(solution)/shard_map/add | solution.py:133
  55.9 0.2 copy.80
  56.0 0.2 copy.81
  56.2 0.7 pad_maximum_fusion
  57.0 7.9 %all-to-all-start = ((f32[2,8,128,32]{2,3,0,1:T(8,128)}), f32[2,8,128,32]{2,3,0,1:T(8,128)S(1)}, u32[]{:S(2)}, u32[]{:S(2)}) async-start(f32[2,8,128,32]{2,3,0,1:T(8,128)} %pad_maximum_fusion), calls=%async_computation | async-start | bytes 524288 | tf_op jit(solution)/shard_map/all_to_all | solution.py:141
  64.8 0.1 multiply_sine_fusion.9
  64.9 0.1 multiply_sine_fusion.8
  64.9 1.7 %copy_bitcast_fusion = f32[2,8,128,32]{2,3,0,1:T(8,128)} fusion(f32[2,1024,32]{1,2,0:T(8,128)} %param.14), kind=kLoop, calls=%fused_computation.36 | loop fusion | bytes 524288 | tf_op jit(solution)/shard_map/reshape | solution.py:138
  66.6 3.8 %all-to-all-done = f32[2,8,128,32]{2,3,0,1:T(8,128)S(1)} async-done(((f32[2,8,128,32]{2,3,0,1:T(8,128)}), f32[2,8,128,32]{2,3,0,1:T(8,128)S(1)}, u32[]{:S(2)}, u32[]{:S(2)}) %all-to-all-start) | async-done | bytes 262176 | tf_op jit(solution)/shard_map/all_to_all | solution.py:141
  70.4 4.6 %all-to-all-start.1 = ((f32[2,8,128,32]{2,3,0,1:T(8,128)}), f32[2,8,128,32]{2,3,0,1:T(8,128)S(1)}, u32[]{:S(2)}, u32[]{:S(2)}) async-start(f32[2,8,128,32]{2,3,0,1:T(8,128)} %copy_bitcast_fusion), calls=%async_computation.1 | async-start | bytes 524288 | tf_op jit(solution)/shard_map/all_to_all | solution.py:142
  75.1 0.1 copy.83
  75.2 0.6 fusion.88
  75.8 0.6 fusion.95
  76.5 4.2 %all-to-all-done.1 = f32[2,8,128,32]{2,3,0,1:T(8,128)S(1)} async-done(((f32[2,8,128,32]{2,3,0,1:T(8,128)}), f32[2,8,128,32]{2,3,0,1:T(8,128)S(1)}, u32[]{:S(2)}, u32[]{:S(2)}) %all-to-all-start.1) | async-done | bytes 262176 | tf_op jit(solution)/shard_map/all_to_all | solution.py:142
  80.8 0.1 copy.91
  80.9 0.6 fusion.92
  81.5 0.6 fusion.85
  82.1 0.1 copy.84
  82.2 0.1 copy.92
  82.4 0.6 convolution_subtract_fusion.4
  83.0 0.6 convolution_add_fusion.4
  83.6 0.6 convolution_add_fusion.5
  84.2 0.8 add_bitcast_fusion
  85.1 0.5 fusion.18
  85.6 0.5 fusion.20
  86.1 0.5 fusion.26
  86.6 0.5 fusion.24
  87.1 0.5 convolution_add_fusion.1
  87.6 0.5 convolution_subtract_fusion.1
  88.2 0.5 convolution_subtract_fusion.2
  88.7 0.5 multiply_add_fusion.2
  89.2 0.5 fusion.40
  89.7 0.5 fusion.36
  90.3 0.5 convolution_subtract_fusion
  90.8 0.5 multiply_add_fusion.1
  91.3 0.6 fusion.32
  91.9 0.6 fusion.30
  92.6 0.6 fusion.8
  93.2 0.1 copy.109
  93.3 0.6 fusion.6
  94.0 0.1 copy.110
  94.1 0.2 maximum_bitcast_fusion
  94.3 9.3 %all_to_all.45 = f32[2,1,128,256]{2,0,1,3:T(2,128)S(1)} all-to-all(f32[2,1,128,256]{2,0,1,3:T(2,128)S(1)} %maximum_bitcast_fusion), channel_id=1, replica_groups=mesh['energy'=8,'space'=4] {'energy'}, dimensions={3} | all-to-all | bytes 524288 | tf_op jit(solution)/shard_map/all_to_all | solution.py:119
  103.7 0.2 copy.108
  103.9 0.7 reshape.95
  (33 shorter events, 0.3 us)
Async XLA Ops:
  0.0 31.3 %copy-start = (f32[2,384,768]{2,1,0:T(8,128)S(1)}, f32[2,384,768]{2,1,0:T(8,128)}, u32[]{:S(2)}) copy-start(f32[2,384,768]{2,1,0:T(8,128)} %param.12) | copy-start | bytes 7077892
  0.0 2.5 %copy-start.1 = (f32[2,384,384]{2,1,0:T(8,128)S(1)}, f32[2,384,384]{2,1,0:T(8,128)}, u32[]{:S(2)}) copy-start(f32[2,384,384]{2,1,0:T(8,128)} %param.10) | copy-start | bytes 3538948
  2.6 3.1 %copy-start.2 = (f32[2,32,384]{2,1,0:T(8,128)S(1)}, f32[2,32,384]{2,1,0:T(8,128)}, u32[]{:S(2)}) copy-start(f32[2,32,384]{2,1,0:T(8,128)} %param.11) | copy-start | bytes 294916
  5.6 25.6 %copy-start.4 = (s32[2,1024]{1,0:T(2,128)S(1)}, s32[2,1024]{1,0:T(2,128)}, u32[]{:S(2)}) copy-start(s32[2,1024]{1,0:T(2,128)} %param.15) | copy-start | bytes 24580
  8.8 5.4 %collective-permute-start = (f32[2,32,384]{2,1,0:T(8,128)S(1)}, f32[2,32,384]{2,1,0:T(8,128)S(1)}, u32[]{:S(2)}, u32[]{:S(2)}) collective-permute-start(f32[2,32,384]{2,1,0:T(8,128)S(1)} %maximum_add_fusion.3), channel_id=1, source_target_pairs={{0,1},{1,2},{2,3},{4,5},{5,6},{6,7},{8,9},{9,10},{10,11},{12,13},{... | collective-permute-start | bytes 294920 | tf_op jit(solution)/shard_map/while/body/eval_jaxpr/ppermute | solution.py:14
  17.3 5.4 %collective-permute-start = (f32[2,32,384]{2,1,0:T(8,128)S(1)}, f32[2,32,384]{2,1,0:T(8,128)S(1)}, u32[]{:S(2)}, u32[]{:S(2)}) collective-permute-start(f32[2,32,384]{2,1,0:T(8,128)S(1)} %maximum_add_fusion.3), channel_id=1, source_target_pairs={{0,1},{1,2},{2,3},{4,5},{5,6},{6,7},{8,9},{9,10},{10,11},{12,13},{... | collective-permute-start | bytes 294920 | tf_op jit(solution)/shard_map/while/body/eval_jaxpr/ppermute | solution.py:14
  25.8 5.4 %collective-permute-start = (f32[2,32,384]{2,1,0:T(8,128)S(1)}, f32[2,32,384]{2,1,0:T(8,128)S(1)}, u32[]{:S(2)}, u32[]{:S(2)}) collective-permute-start(f32[2,32,384]{2,1,0:T(8,128)S(1)} %maximum_add_fusion.3), channel_id=1, source_target_pairs={{0,1},{1,2},{2,3},{4,5},{5,6},{6,7},{8,9},{9,10},{10,11},{12,13},{... | collective-permute-start | bytes 294920 | tf_op jit(solution)/shard_map/while/body/eval_jaxpr/ppermute | solution.py:14
  31.2 1.7 %copy-start.3 = (f32[2,768,32]{1,2,0:T(8,128)S(1)}, f32[2,768,32]{1,2,0:T(8,128)}, u32[]{:S(2)}) copy-start(f32[2,768,32]{1,2,0:T(8,128)} %param.13) | copy-start | bytes 589828
  57.0 13.5 %all-to-all-start = ((f32[2,8,128,32]{2,3,0,1:T(8,128)}), f32[2,8,128,32]{2,3,0,1:T(8,128)S(1)}, u32[]{:S(2)}, u32[]{:S(2)}) async-start(f32[2,8,128,32]{2,3,0,1:T(8,128)} %pad_maximum_fusion), calls=%async_computation | async-start | bytes 524288 | tf_op jit(solution)/shard_map/all_to_all | solution.py:141
  70.4 10.3 %all-to-all-start.1 = ((f32[2,8,128,32]{2,3,0,1:T(8,128)}), f32[2,8,128,32]{2,3,0,1:T(8,128)S(1)}, u32[]{:S(2)}, u32[]{:S(2)}) async-start(f32[2,8,128,32]{2,3,0,1:T(8,128)} %copy_bitcast_fusion), calls=%async_computation.1 | async-start | bytes 524288 | tf_op jit(solution)/shard_map/all_to_all | solution.py:142
where the time goes:
time: 107 us; the launch traced here: 105 us
  matrix products  24.6 us (23%)
  local copies, waits for them, and re-layouts  21.7 us (20%)
  waiting for transfers between devices  20.2 us (19%)
  starting transfers between devices  16.4 us (15%)
  other arithmetic  11.8 us (11%)
  blocking collectives  9.34 us (9%)
    dot_general x24, matrix products, single(): jnp.einsum(pattern, first_part, second_part, precision=highest, preferred...  13.8 us
    ppermute x3, waiting for transfers between devices, shifted_2(): return lax.ppermute(x, axis, pairs)  12.2 us
    all_to_all x1, blocking collectives, correlate(): lax.all_to_all(response, 'energy', split_axis=3, concat_axis=1, tiled=True)  9.34 us
    dot_general x3, matrix products, stacked_step(): jnp.dot(joined, coupled, precision=highest, preferred_element_type=jnp.fl...  9.27 us
    all_to_all x1, starting transfers between devices, body(): lax.all_to_all(lesser, 'energy', split_axis=1, concat_axis=3, tiled=True)  7.86 us
    gather x1, local copies, waits for them, and re-layouts, body(): left_rows = jnp.take(wavefunction, element_pairs[0], axis=1)  7.5 us
    gather x1, local copies, waits for them, and re-layouts, body(): right_rows = jnp.take(wavefunction, element_pairs[1], axis=1)  7.49 us
    select_n x1, other arithmetic, body(): right_rows = jnp.take(wavefunction, element_pairs[1], axis=1)  6.09 us
  transfers between devices with their start and end apart: 5, of which 5 were waited for; matrix products, arithmetic and copies ran while one was open for 3% of the time, Pallas kernels for 0%

commit v1 on v0

v1 whole, which is shorter than its diff:
```python
import functools
import math

import jax
import jax.numpy as jnp
import ml_dtypes
import numpy as np
from jax import lax
from jax.experimental import pallas as pl
from jax.experimental.pallas import tpu as pltpu
from jax.sharding import PartitionSpec as P

LANES = 128
RADIX = 256
MESH = pl.DeviceIdType.MESH
bf16, f32 = jnp.bfloat16, jnp.float32


def split(x):
    high = x.astype(bf16)
    return high, (x - high.astype(f32)).astype(bf16)


def mm(a, b):
    return jnp.dot(a, b, preferred_element_type=f32)


def transform_tables(length):
    inner = min(length, RADIX)
    index = np.arange(inner)
    angle = 2.0 * np.pi / inner * (np.outer(index, index) % inner)
    table = np.concatenate([np.cos(angle), np.sin(angle)], axis=0).astype(np.float32)
    high = table.astype(ml_dtypes.bfloat16)
    low = (table - high.astype(np.float32)).astype(ml_dtypes.bfloat16)
    return np.concatenate([high, high, low], axis=1)


def small_transform(table, x, sign):
    inner, width = x.shape[0], x.shape[1] // 2
    high, low = split(x)
    product = mm(table, jnp.concatenate([high, low, high], axis=0))
    cos, sin = product[:inner], product[inner:]
    re = cos[:, :width] - sign * sin[:, width:]
    im = cos[:, width:] + sign * sin[:, :width]
    return re, im


def twiddle(k, inner, length, sign):
    row = lax.broadcasted_iota(jnp.int32, (inner, 1), 0)
    angle = (sign * 2.0 * math.pi / length) * ((row * k) % length).astype(f32)
    return jnp.cos(angle), jnp.sin(angle)


def combine(parts, k, sign):
    total_re = total_im = None
    for a, (re, im) in enumerate(parts):
        angle = sign * 2.0 * math.pi * (a * k % len(parts)) / len(parts)
        c, s = math.cos(angle), math.sin(angle)
        one_re, one_im = c * re - s * im, c * im + s * re
        total_re = one_re if a == 0 else total_re + one_re
        total_im = one_im if a == 0 else total_im + one_im
    return total_re, total_im


def forward(table, parts, length):
    outer, inner = len(parts), parts[0][0].shape[0]
    out = []
    for k in range(outer):
        re, im = parts[0] if outer == 1 else combine(parts, k, -1.0)
        if k:
            c, s = twiddle(k, inner, length, -1.0)
            re, im = c * re - s * im, c * im + s * re
        out.append(small_transform(table, jnp.concatenate([re, im], axis=1), -1.0))
    return out


def inverse(table, spectra, length):
    outer, inner = len(spectra), spectra[0][0].shape[0]
    parts = []
    for k, (re, im) in enumerate(spectra):
        re, im = small_transform(table, jnp.concatenate([re, im], axis=1), 1.0)
        if k:
            c, s = twiddle(k, inner, length, 1.0)
            re, im = c * re - s * im, c * im + s * re
        parts.append((re, im))
    if outer == 1:
        return parts
    return [combine(parts, a, 1.0) for a in range(outer)]


def apply_map(states, high_ref, low_ref):
    count = states.shape[0] // 2
    high, low = split(states)
    rows = jnp.concatenate([high, low], axis=0)
    planes = []
    for plane in range(2):
        p = mm(rows, high_ref[plane])
        planes.append(p[: 2 * count] + p[2 * count :] + mm(high, low_ref[plane]))
    re = planes[0][:count] - planes[1][count:]
    im = planes[1][:count] + planes[0][count:]
    return re, im


def kernel(
    groups, space,
    chain_hbm, source_ref, map_hbm, local_ref, inter_ref, pairs_ref, table_hbm,
    out_ref,
    chain_f, map_f, table, chain_hi, chain_lo, map_hi, map_lo, onehot,
    incoming, outgoing, i_stage, i_recv, l_stage, l_recv, r_stage, r_recv,
    load_sem, hop_send, hop_recv, i_send, i_got, l_send, l_got, r_send, r_got,
):
    me = lax.axis_index("energy")
    z = lax.axis_index("space")
    count = source_ref.shape[1]
    width = local_ref.shape[2]
    selected = inter_ref.shape[2]
    piece = selected // groups
    chunk = l_stage.shape[3]
    per = chunk // piece
    chunks = selected // chunk
    length = groups * count

    loads = [
        pltpu.make_async_copy(s, d, load_sem.at[i])
        for i, (s, d) in enumerate(((chain_hbm, chain_f), (map_hbm, map_f), (table_hbm, table)))
    ]
    for load in loads:
        load.start()

    barrier = pltpu.get_barrier_semaphore()
    for d in range(1, groups):
        pl.semaphore_signal(
            barrier, inc=1, device_id=(lax.rem(me + d, groups), z), device_id_type=MESH
        )

    @pl.when(z > 0)
    def _():
        pl.semaphore_signal(barrier, inc=1, device_id=(me, z - 1), device_id_type=MESH)

    @pl.when(z < space - 1)
    def _():
        pl.semaphore_signal(barrier, inc=1, device_id=(me, z + 1), device_id_type=MESH)

    if piece < chunk:
        for ref in (i_stage, l_stage, i_recv, l_recv):
            ref[...] = jnp.zeros_like(ref)
    for g in range(groups):
        i_stage[g, :, :, :piece] = inter_ref[:, :, g * piece : (g + 1) * piece]
    i_recv[me] = i_stage[me]

    beside = jnp.where(z > 0, 1, 0) + jnp.where(z < space - 1, 1, 0)
    pl.semaphore_wait(barrier, groups - 1 + beside)

    def hop(src):
        return pltpu.make_async_remote_copy(
            src_ref=src, dst_ref=incoming, send_sem=hop_send, recv_sem=hop_recv,
            device_id=(me, z + 1), device_id_type=MESH,
        )

    def exchange(stage, recv, send_sem, recv_sem, peer):
        return pltpu.make_async_remote_copy(
            src_ref=stage.at[peer], dst_ref=recv.at[me], send_sem=send_sem.at[peer],
            recv_sem=recv_sem.at[me], device_id=(peer, z), device_id_type=MESH,
        )

    def arrival(stage, recv, send_sem, recv_sem, peer):
        return pltpu.make_async_remote_copy(
            src_ref=stage.at[peer], dst_ref=recv.at[peer], send_sem=send_sem.at[peer],
            recv_sem=recv_sem.at[peer], device_id=(peer, z), device_id_type=MESH,
        )

    @pl.when(z == 0)
    def _():
        outgoing[...] = source_ref[...]
        hop(outgoing).start()

    for d in range(1, groups):
        exchange(i_stage, i_recv, i_send, i_got, lax.rem(me + d, groups)).start()

    def prepare():
        loads[1].wait()
        for plane in range(2):
            map_hi[plane], map_lo[plane] = split(map_f[plane])
        row = lax.broadcasted_iota(jnp.int32, (width, chunk), 0)
        for c in range(chunks):
            for side in range(2):
                index = pairs_ref[side : side + 1, c * chunk : (c + 1) * chunk]
                onehot[c, :, side * chunk : (side + 1) * chunk] = jnp.where(
                    row == index, 1.0, 0.0
                ).astype(bf16)

    loads[0].wait()
    for plane in range(2):
        chain_hi[plane], chain_lo[plane] = split(chain_f[plane])

    @pl.when(z >= 2)
    def _():
        prepare()

    @pl.when(z == 0)
    def _():
        incoming[...] = jnp.zeros_like(incoming)

    @pl.when(z > 0)
    def _():
        hop(outgoing).wait_recv()

    def joined():
        return jnp.concatenate([incoming[0], incoming[1]], axis=0)

    @pl.when(jnp.logical_and(z > 0, z < space - 1))
    def _():
        re, im = apply_map(joined(), chain_hi, chain_lo)
        outgoing[0] = re + source_ref[0]
        outgoing[1] = im + source_ref[1]
        hop(outgoing).start()

    @pl.when(z < 2)
    def _():
        prepare()

    re, im = apply_map(joined(), map_hi, map_lo)
    waves = jnp.concatenate([re + local_ref[0], im + local_ref[1]], axis=0)
    rows = jnp.concatenate(split(waves), axis=0)

    for d in range(chunks):
        c = lax.rem((me * piece) // chunk + 1 + d, chunks)
        both = mm(rows, onehot[c])
        both = both[: 2 * count] + both[2 * count :]
        left_re, left_im = both[:count, :chunk], both[count:, :chunk]
        right_re, right_im = both[:count, chunk:], both[count:, chunk:]
        lesser_re = left_re * right_re + left_im * right_im
        lesser_im = left_im * right_re - left_re * right_im
        for j in range(per):
            g = c * per + j
            part = slice(j * piece, (j + 1) * piece)
            l_stage[g, 0, :, :piece] = lesser_re[:, part]
            l_stage[g, 1, :, :piece] = lesser_im[:, part]

            @pl.when(g != me)
            def _():
                exchange(l_stage, l_recv, l_send, l_got, g).start()

            @pl.when(g == me)
            def _():
                l_recv[me] = l_stage[me]

    inner = min(length, RADIX)

    def gathered(recv):
        planes = [recv[:, plane].reshape(length, chunk) for plane in range(2)]
        return [
            (planes[0][a * inner : (a + 1) * inner], planes[1][a * inner : (a + 1) * inner])
            for a in range(length // inner)
        ]

    loads[2].wait()
    for d in range(1, groups):
        arrival(i_stage, i_recv, i_send, i_got, lax.rem(me + groups - d, groups)).wait_recv()
    screened = forward(table[...], gathered(i_recv), length)

    for d in range(1, groups):
        arrival(l_stage, l_recv, l_send, l_got, lax.rem(me + groups - d, groups)).wait_recv()
    lesser = forward(table[...], gathered(l_recv), length)
    spectra = [
        (a * c - b * d, a * d + b * c) for (a, b), (c, d) in zip(lesser, screened)
    ]
    response = inverse(table[...], spectra, length)
    factor = length**-1.5
    share = inner // count
    for a, pair in enumerate(response):
        for plane in range(2):
            r_stage[a * share : (a + 1) * share, plane] = (pair[plane] * factor).reshape(
                share, count, chunk
            )
    for d in range(1, groups):
        exchange(r_stage, r_recv, r_send, r_got, lax.rem(me + d, groups)).start()
    r_recv[me] = r_stage[me]
    for d in range(1, groups):
        arrival(r_stage, r_recv, r_send, r_got, lax.rem(me + groups - d, groups)).wait_recv()
    for g in range(groups):
        out_ref[:, :, g * piece : (g + 1) * piece] = r_recv[g, :, :, :piece]

    for d in range(1, groups):
        peer = lax.rem(me + d, groups)
        exchange(i_stage, i_recv, i_send, i_got, peer).wait_send()
        exchange(l_stage, l_recv, l_send, l_got, peer).wait_send()
        exchange(r_stage, r_recv, r_send, r_got, peer).wait_send()

    @pl.when(z < space - 1)
    def _():
        hop(outgoing).wait_send()


def body(groups, space, chain_map, chain_source, local_map, local_source, interaction, element_pairs):
    count = chain_source.shape[1]
    block = chain_map.shape[2]
    width = local_map.shape[2]
    selected = interaction.shape[1]
    chunk = max(LANES, selected // groups)
    table = jnp.asarray(transform_tables(groups * count))
    exchanged = pltpu.VMEM((groups, 2, count, chunk), f32)
    vmem = pl.BlockSpec(memory_space=pltpu.VMEM)
    hbm = pl.BlockSpec(memory_space=pl.ANY)
    dma = pltpu.SemaphoreType.DMA
    out = pl.pallas_call(
        functools.partial(kernel, groups, space),
        out_shape=jax.ShapeDtypeStruct((2, count, selected), f32),
        in_specs=[hbm, vmem, hbm, vmem, vmem, vmem, hbm],
        out_specs=vmem,
        scratch_shapes=[
            pltpu.VMEM(chain_map.shape, f32),
            pltpu.VMEM(local_map.shape, f32),
            pltpu.VMEM(table.shape, bf16),
            pltpu.VMEM(chain_map.shape, bf16),
            pltpu.VMEM(chain_map.shape, bf16),
            pltpu.VMEM(local_map.shape, bf16),
            pltpu.VMEM(local_map.shape, bf16),
            pltpu.VMEM((selected // chunk, width, 2 * chunk), bf16),
            pltpu.VMEM((2, count, block), f32),
            pltpu.VMEM((2, count, block), f32),
            *[exchanged] * 6,
            dma((3,)),
            dma,
            dma,
            *[dma((groups,))] * 6,
        ],
        compiler_params=pltpu.CompilerParams(
            collective_id=0, has_side_effects=True, vmem_limit_bytes=56 * 2**20
        ),
    )(
        chain_map,
        chain_source,
        local_map,
        jnp.swapaxes(local_source, 1, 2),
        jnp.swapaxes(interaction, 1, 2),
        element_pairs,
        table,
    )
    return jnp.swapaxes(out, 1, 2)


def solution(mesh):
    in_specs = (
        P(None, "space", None),
        P(None, "energy", "space"),
        P(None, "space", None),
        P(None, "space", "energy"),
        P(None, "space", "energy"),
        P(None, "space"),
    )
    out_specs = P(None, "space", "energy")
    run = functools.partial(body, mesh.shape["energy"], mesh.shape["space"])
    return jax.shard_map(run, mesh=mesh, in_specs=in_specs, out_specs=out_specs, check_vma=False)
```

time: 107 us -> 27.9 us (0.26); the launches traced: 105 us -> 27.7 us
  Pallas kernels: 0 us -> 26 us
  matrix products: 24.6 us -> 0 us
  waiting for transfers between devices: 20.2 us -> 0 us
  local copies, waits for them, and re-layouts: 21.7 us -> 1.67 us
  starting transfers between devices: 16.4 us -> 0 us
  other arithmetic: 11.8 us -> 0 us
  blocking collectives: 9.34 us -> 0 us
    pallas_call x0 -> x1, Pallas kernels: none -> 26 us  [body(): pl.pallas_call(functools.partial(kernel, groups, space), out_shape=jax.Sh...]
    dot_general x28 -> x0, matrix products: 24.6 us -> none  [the longest x24 13.8 us: single(): jnp.einsum(pattern, first_part, second_part, precision=highest, preferred...]
    gather x2 -> x0, local copies, waits for them, and re-layouts: 15 us -> none  [the longest x1 7.5 us: body(): left_rows = jnp.take(wavefunction, element_pairs[0], axis=1)]
    all_to_all x2 -> x0, starting transfers between devices: 12.5 us -> none  [the longest x1 7.86 us: body(): lax.all_to_all(lesser, 'energy', split_axis=1, concat_axis=3, tiled=True)]
    ppermute x3 -> x0, waiting for transfers between devices: 12.2 us -> none  [shifted_2(): return lax.ppermute(x, axis, pairs)]
    all_to_all x1 -> x0, blocking collectives: 9.34 us -> none  [correlate(): lax.all_to_all(response, 'energy', split_axis=3, concat_axis=1, tiled=True)]
    all_to_all x2 -> x0, waiting for transfers between devices: 8.06 us -> none  [the longest x1 4.24 us: body(): lax.all_to_all(screened, 'energy', split_axis=1, concat_axis=3, tiled=True)]
    select_n x1 -> x0, other arithmetic: 6.09 us -> none  [body(): right_rows = jnp.take(wavefunction, element_pairs[1], axis=1)]
  transfers between devices with their start and end apart: 5 -> 0, of which waited for: 5 -> 0; matrix products, arithmetic and copies ran while one was open for 3% -> 0% of each run, Pallas kernels for 0% -> 0%
where the time goes in v1:
time: 27.9 us; the launch traced here: 27.7 us
  Pallas kernels  26 us (93%)
  local copies, waits for them, and re-layouts  1.67 us (6%)
    pallas_call x1, Pallas kernels, body(): pl.pallas_call(functools.partial(kernel, groups, space), out_shape=jax.Sh...  26 us
    unnamed x1, local copies, waits for them, and re-layouts  1.67 us

profile of v1, /device:TPU:25, one launch (start us, length us, event | category | flops | bytes accessed | tf_op | source)
XLA Modules:
  0.0 27.7 jit_solution(17303910238735553790)
XLA Ops:
  0.0 26.0 %shard_map.73 = f32[2,32,1024]{2,1,0:T(8,128)} custom-call(f32[2,384,384]{2,1,0:T(8,128)} %chain_hbm.1, f32[2,32,384]{2,1,0:T(8,128)} %source_ref.1, f32[2,384,768]{2,1,0:T(8,128)} %map_hbm.1, f32[2,32,768]{2,1,0:T(8,128)} %bitcast.5, f32[2,32,1024]{2,1,0:T(8,128)} %bitcast.4, s32[2,1024]{1,0:T(2,128)} %pairs_ref.1, bf16[512,768]{1,0:T(8,128)(2,1)} %constant.2.clone.table_hbm), custom_call_target="tpu_custom_call" | custom-call | tf_op jit(solution)/shard_map/pallas_call | solution.py:306
  26.1 1.7 %copy.9 = f32[2,1024,32]{1,2,0:T(8,128)} copy(f32[2,1024,32]{1,2,0:T(8,128)} %bitcast.3) | data formatting | bytes 524288

commit v2 on v1

--- a/solution.py
+++ b/solution.py
@@ -119,6 +119,7 @@
     per = chunk // piece
     chunks = selected // chunk
     length = groups * count
+    cores = 2 if chunks % 2 == 0 else 1
 
     loads = [
         pltpu.make_async_copy(s, d, load_sem.at[i])
@@ -151,10 +152,13 @@
     beside = jnp.where(z > 0, 1, 0) + jnp.where(z < space - 1, 1, 0)
     pl.semaphore_wait(barrier, groups - 1 + beside)
 
-    def hop(src):
+    turns = incoming.shape[0]
+    step = count // turns
+
+    def hop(t):
         return pltpu.make_async_remote_copy(
-            src_ref=src, dst_ref=incoming, send_sem=hop_send, recv_sem=hop_recv,
-            device_id=(me, z + 1), device_id_type=MESH,
+            src_ref=outgoing.at[t], dst_ref=incoming.at[t], send_sem=hop_send.at[t],
+            recv_sem=hop_recv.at[t], device_id=(me, z + 1), device_id_type=MESH,
         )
 
     def exchange(stage, recv, send_sem, recv_sem, peer):
@@ -171,8 +175,9 @@
 
     @pl.when(z == 0)
     def _():
-        outgoing[...] = source_ref[...]
-        hop(outgoing).start()
+        for t in range(turns):
+            outgoing[t] = source_ref[:, t * step : (t + 1) * step]
+            hop(t).start()
 
     for d in range(1, groups):
         exchange(i_stage, i_recv, i_send, i_got, lax.rem(me + d, groups)).start()
@@ -201,30 +206,33 @@
     def _():
         incoming[...] = jnp.zeros_like(incoming)
 
-    @pl.when(z > 0)
-    def _():
-        hop(outgoing).wait_recv()
-
-    def joined():
-        return jnp.concatenate([incoming[0], incoming[1]], axis=0)
-
     @pl.when(jnp.logical_and(z > 0, z < space - 1))
     def _():
-        re, im = apply_map(joined(), chain_hi, chain_lo)
-        outgoing[0] = re + source_ref[0]
-        outgoing[1] = im + source_ref[1]
-        hop(outgoing).start()
+        for t in range(turns):
+            hop(t).wait_recv()
+            states = jnp.concatenate([incoming[t, 0], incoming[t, 1]], axis=0)
+            re, im = apply_map(states, chain_hi, chain_lo)
+            outgoing[t, 0] = re + source_ref[0, t * step : (t + 1) * step]
+            outgoing[t, 1] = im + source_ref[1, t * step : (t + 1) * step]
+            hop(t).start()
+
+    @pl.when(jnp.logical_and(z > 0, z == space - 1))
+    def _():
+        for t in range(turns):
+            hop(t).wait_recv()
 
     @pl.when(z < 2)
     def _():
         prepare()
 
-    re, im = apply_map(joined(), map_hi, map_lo)
+    joined = [incoming[t, plane] for plane in range(2) for t in range(turns)]
+    re, im = apply_map(jnp.concatenate(joined, axis=0), map_hi, map_lo)
     waves = jnp.concatenate([re + local_ref[0], im + local_ref[1]], axis=0)
     rows = jnp.concatenate(split(waves), axis=0)
 
     for d in range(chunks):
-        c = lax.rem((me * piece) // chunk + 1 + d, chunks)
+        pair = lax.rem((me * piece) // (chunk * cores) + 1 + d // cores, chunks // cores)
+        c = pair * cores + d % cores
         both = mm(rows, onehot[c])
         both = both[: 2 * count] + both[2 * count :]
         left_re, left_im = both[:count, :chunk], both[count:, :chunk]
@@ -289,7 +297,8 @@
 
     @pl.when(z < space - 1)
     def _():
-        hop(outgoing).wait_send()
+        for t in range(turns):
+            hop(t).wait_send()
 
 
 def body(groups, space, chain_map, chain_source, local_map, local_source, interaction, element_pairs):
@@ -299,9 +308,10 @@
     selected = interaction.shape[1]
     chunk = max(LANES, selected // groups)
     table = jnp.asarray(transform_tables(groups * count))
+    turns = 2 if count % 16 == 0 else 1
     exchanged = pltpu.VMEM((groups, 2, count, chunk), f32)
     vmem = pl.BlockSpec(memory_space=pltpu.VMEM)
-    hbm = pl.BlockSpec(memory_space=pl.ANY)
+    hbm = pl.BlockSpec(memory_space=pltpu.MemorySpace.HBM)
     dma = pltpu.SemaphoreType.DMA
     out = pl.pallas_call(
         functools.partial(kernel, groups, space),
@@ -317,16 +327,16 @@
             pltpu.VMEM(local_map.shape, bf16),
             pltpu.VMEM(local_map.shape, bf16),
             pltpu.VMEM((selected // chunk, width, 2 * chunk), bf16),
-            pltpu.VMEM((2, count, block), f32),
-            pltpu.VMEM((2, count, block), f32),
+            pltpu.VMEM((turns, 2, count // turns, block), f32),
+            pltpu.VMEM((turns, 2, count // turns, block), f32),
             *[exchanged] * 6,
             dma((3,)),
-            dma,
-            dma,
+            dma((turns,)),
+            dma((turns,)),
             *[dma((groups,))] * 6,
         ],
         compiler_params=pltpu.CompilerParams(
-            collective_id=0, has_side_effects=True, vmem_limit_bytes=56 * 2**20
+            collective_id=0, has_side_effects=True, vmem_limit_bytes=53 * 2**20
         ),
     )(
         chain_map,

time: 27.9 us -> 27.4 us (0.982)
  Pallas kernels: 26 us -> 23 us
  local copies, waits for them, and re-layouts: 1.67 us -> 4.17 us
    pallas_call x1, Pallas kernels: 26 us -> 23 us  [body(): pl.pallas_call(functools.partial(kernel, groups, space), out_shape=jax.Sh...]
    unnamed x1 -> x9, local copies, waits for them, and re-layouts: 1.67 us -> 4.17 us
where the time goes in v2:
time: 27.4 us; the launch traced here: 27.1 us
  Pallas kernels  23 us (84%)
  local copies, waits for them, and re-layouts  4.17 us (15%)
    pallas_call x1, Pallas kernels, body(): pl.pallas_call(functools.partial(kernel, groups, space), out_shape=jax.Sh...  23 us
    unnamed x9, local copies, waits for them, and re-layouts  4.17 us

profile of v2, /device:TPU:25, one launch (start us, length us, event | category | flops | bytes accessed | tf_op | source)
XLA Modules:
  0.0 27.1 jit_solution(1660762540094574442)
XLA Ops:
  0.0 0.0 copy-start
  0.0 0.9 %copy-done = f32[2,1024,32]{1,2,0:T(8,128)S(1)} copy-done((f32[2,1024,32]{1,2,0:T(8,128)S(1)}, f32[2,1024,32]{1,2,0:T(8,128)}, u32[]{:S(2)}) %copy-start) | copy-done | bytes 262168
  1.0 0.0 copy-start.1
  1.0 0.9 %copy-done.1 = f32[2,768,32]{1,2,0:T(8,128)S(1)} copy-done((f32[2,768,32]{1,2,0:T(8,128)S(1)}, f32[2,768,32]{1,2,0:T(8,128)}, u32[]{:S(2)}) %copy-start.1) | copy-done | bytes 196632
  1.9 0.0 copy-start.2
  1.9 0.9 %copy-done.2 = f32[2,32,384]{2,1,0:T(8,128)S(1)} copy-done((f32[2,32,384]{2,1,0:T(8,128)S(1)}, f32[2,32,384]{2,1,0:T(8,128)}, u32[]{:S(2)}) %copy-start.2) | copy-done | bytes 98328
  2.8 0.0 copy-start.3
  2.8 0.7 %copy-done.3 = s32[2,1024]{1,0:T(2,128)S(1)} copy-done((s32[2,1024]{1,0:T(2,128)S(1)}, s32[2,1024]{1,0:T(2,128)}, u32[]{:S(2)}) %copy-start.3) | copy-done | bytes 8216
  3.5 23.0 %shard_map.73 = f32[2,32,1024]{2,1,0:T(8,128)S(1)} custom-call(f32[2,384,384]{2,1,0:T(8,128)} %chain_hbm.1, f32[2,32,384]{2,1,0:T(8,128)S(1)} %copy-done.2, f32[2,384,768]{2,1,0:T(8,128)} %map_hbm.1, f32[2,32,768]{2,1,0:T(8,128)S(1)} %bitcast.5, f32[2,32,1024]{2,1,0:T(8,128)S(1)} %bitcast.4, s32[2,1024]{1,0:T(2,128)S(1)} %copy-done.3, ...), custom_call_target="tpu_custom_call" | custom-call | tf_op jit(solution)/shard_map/pallas_call | solution.py:316
  26.4 0.7 %copy.9 = f32[2,1024,32]{1,2,0:T(8,128)} copy(f32[2,1024,32]{1,2,0:T(8,128)S(1)} %bitcast.3) | data formatting | bytes 524288
Async XLA Ops:
  0.0 0.9 %copy-start = (f32[2,1024,32]{1,2,0:T(8,128)S(1)}, f32[2,1024,32]{1,2,0:T(8,128)}, u32[]{:S(2)}) copy-start(f32[2,1024,32]{1,2,0:T(8,128)} %param.11) | copy-start | bytes 786436
  1.0 0.9 %copy-start.1 = (f32[2,768,32]{1,2,0:T(8,128)S(1)}, f32[2,768,32]{1,2,0:T(8,128)}, u32[]{:S(2)}) copy-start(f32[2,768,32]{1,2,0:T(8,128)} %param.10) | copy-start | bytes 589828
  1.9 0.9 %copy-start.2 = (f32[2,32,384]{2,1,0:T(8,128)S(1)}, f32[2,32,384]{2,1,0:T(8,128)}, u32[]{:S(2)}) copy-start(f32[2,32,384]{2,1,0:T(8,128)} %source_ref.1) | copy-start | bytes 294916
  2.8 0.7 %copy-start.3 = (s32[2,1024]{1,0:T(2,128)S(1)}, s32[2,1024]{1,0:T(2,128)}, u32[]{:S(2)}) copy-start(s32[2,1024]{1,0:T(2,128)} %pairs_ref.1) | copy-start | bytes 24580

commit v3 on v2

--- a/solution.py
+++ b/solution.py
@@ -336,7 +336,7 @@
             *[dma((groups,))] * 6,
         ],
         compiler_params=pltpu.CompilerParams(
-            collective_id=0, has_side_effects=True, vmem_limit_bytes=53 * 2**20
+            collective_id=0, has_side_effects=True, vmem_limit_bytes=56 * 2**20
         ),
     )(
         chain_map,

time: 27.4 us -> 26.6 us (0.971)
  local copies, waits for them, and re-layouts: 4.17 us -> 1.67 us
  Pallas kernels: 23 us -> 24.8 us
    unnamed x9 -> x1, local copies, waits for them, and re-layouts: 4.17 us -> 1.67 us
    pallas_call x1, Pallas kernels: 23 us -> 24.8 us  [body(): pl.pallas_call(functools.partial(kernel, groups, space), out_shape=jax.Sh...]
where the time goes in v3:
time: 26.6 us; the launch traced here: 26.4 us
  Pallas kernels  24.8 us (93%)
  local copies, waits for them, and re-layouts  1.67 us (6%)
    pallas_call x1, Pallas kernels, body(): pl.pallas_call(functools.partial(kernel, groups, space), out_shape=jax.Sh...  24.8 us
    unnamed x1, local copies, waits for them, and re-layouts  1.67 us

profile of v3, /device:TPU:25, one launch (start us, length us, event | category | flops | bytes accessed | tf_op | source)
XLA Modules:
  0.0 26.4 jit_solution(1338276066660585986)
XLA Ops:
  0.0 24.8 %shard_map.73 = f32[2,32,1024]{2,1,0:T(8,128)} custom-call(f32[2,384,384]{2,1,0:T(8,128)} %chain_hbm.1, f32[2,32,384]{2,1,0:T(8,128)} %source_ref.1, f32[2,384,768]{2,1,0:T(8,128)} %map_hbm.1, f32[2,32,768]{2,1,0:T(8,128)} %bitcast.5, f32[2,32,1024]{2,1,0:T(8,128)} %bitcast.4, s32[2,1024]{1,0:T(2,128)} %pairs_ref.1, bf16[512,768]{1,0:T(8,128)(2,1)} %constant.2.clone.table_hbm), custom_call_target="tpu_custom_call" | custom-call | tf_op jit(solution)/shard_map/pallas_call | solution.py:316
  24.8 1.7 %copy.9 = f32[2,1024,32]{1,2,0:T(8,128)} copy(f32[2,1024,32]{1,2,0:T(8,128)} %bitcast.3) | data formatting | bytes 524288
